TPU v7x, 128 devices: a whole 4x4x4 slice. The times are simulated.
128 devices in a mesh: inp: 4 (over z_lo, core), out: 4 (over x), dep: 8 (over y, z_hi).
Axes of the slice: x: 4, y: 4, z: 4 (z_hi: 2, z_lo: 2; z = z_hi * 2 + z_lo), core: 2. Of those that a mesh axis runs over, the one named last changes fastest.
Arguments:
- tokens: bfloat16 [512, 8192], P(('out', 'dep'), 'inp'), may hold values from -6 to 6
- cotangent: bfloat16 [512, 8192], P(('out', 'dep'), 'inp'), may hold values from -6 to 6
- gate_weight: bfloat16 [8192, 28672], P('inp', ('out', 'dep')), may hold values from -0.0625 to 0.0625
- up_weight: bfloat16 [8192, 28672], P('inp', ('out', 'dep')), may hold values from -0.0625 to 0.0625
- down_weight: bfloat16 [28672, 8192], P(('out', 'dep'), 'inp'), may hold values from -0.03125 to 0.03125
- seq_ids: int32 [512], P(('out', 'dep')), may hold values from 0 to 15, never falling along the last dimension, each value on 1 to 64 neighbouring positions
- chosen: int32 [512], P(('out', 'dep')), may hold values 0 or 1
- margins: float32 [16], replicated, may hold values from -3 to 3
- counts: int32 [32], replicated, may hold values from 32 to 256
Outputs:
- grad_input: bfloat16 [512, 8192], P(('out', 'dep'), 'inp')
- grad_gate: bfloat16 [8192, 28672], P('inp', ('out', 'dep'))
- grad_up: bfloat16 [8192, 28672], P('inp', ('out', 'dep'))
- grad_down: bfloat16 [28672, 8192], P(('out', 'dep'), 'inp')
Inputs may be any that keep to these rules, and one draw needn't show every extreme that they name: `seq_ids`: a pair's tokens stand in one run; ids never fall along the tokens.
All inputs are finite; a program needn't handle non-finite values. No bound on the sum of `chosen` on one device may be relied on, other than what follows from the above.
Results may differ from a plain program's by a relative error of at most 0.0058.
Values may be sent and summed in bfloat16 or wider, within the bound.
A program may use at most 128 MiB of HBM per device.

v0:
```python
import jax
import jax.numpy as jnp
from jax import lax
from jax.sharding import PartitionSpec as P

SIMPO_BETA = 2.5
LOSS_SCALE = 64.0


def token_weights(seq_ids, chosen, margins, counts):
    pair_count = margins.shape[0]
    pair_hot = (seq_ids[:, None] == jnp.arange(pair_count, dtype=jnp.int32)[None, :]).astype(
        jnp.float32
    )
    response = 2 * seq_ids + chosen
    response_hot = (
        response[:, None] == jnp.arange(2 * pair_count, dtype=jnp.int32)[None, :]
    ).astype(jnp.float32)
    margin_tok = jnp.sum(pair_hot * margins[None, :], axis=1)
    length_tok = jnp.sum(response_hot * counts.astype(jnp.float32)[None, :], axis=1)
    polarity = 1.0 - 2.0 * chosen.astype(jnp.float32)
    return polarity * SIMPO_BETA * LOSS_SCALE * jax.nn.sigmoid(-margin_tok) / length_tok


def activate(gate_sum, up_sum):
    logistic = jax.nn.sigmoid(gate_sum)
    swish = gate_sum * logistic
    return (logistic, swish, (swish * up_sum).astype(jnp.bfloat16))


def act_grads(hidden_grad, gate_sum, up_sum, logistic, swish):
    gate_grad = (hidden_grad * up_sum * logistic * (1.0 + gate_sum * (1.0 - logistic))).astype(
        jnp.bfloat16
    )
    up_grad = (hidden_grad * swish).astype(jnp.bfloat16)
    return (gate_grad, up_grad)


def contract_rows(left, right):
    return lax.dot_general(
        left, right, (((0,), (0,)), ((), ())), preferred_element_type=jnp.float32
    )


def contract_cols(left, right):
    return lax.dot_general(
        left, right, (((1,), (1,)), ((), ())), preferred_element_type=jnp.float32
    )


def on_device(
    tokens, cotangent, gate_weight, up_weight, down_weight, seq_ids, chosen, margins, counts
):
    token_weight = token_weights(seq_ids, chosen, margins, counts)
    local_grad = (cotangent.astype(jnp.float32) * token_weight[:, None]).astype(jnp.bfloat16)
    inputs = lax.all_gather(tokens, ("out", "dep"), axis=0, tiled=True)
    gate_part = jnp.dot(inputs, gate_weight, preferred_element_type=jnp.float32)
    up_part = jnp.dot(inputs, up_weight, preferred_element_type=jnp.float32)
    gate_sum, up_sum = lax.psum((gate_part, up_part), "inp")
    logistic, swish, hidden = activate(gate_sum, up_sum)
    out_grad = lax.all_gather(local_grad, ("out", "dep"), axis=0, tiled=True)
    hidden_part = contract_cols(out_grad, down_weight)
    hidden_grad = lax.psum(hidden_part, "inp")
    gate_grad, up_grad = act_grads(hidden_grad, gate_sum, up_sum, logistic, swish)
    grad_down = contract_rows(hidden, out_grad).astype(jnp.bfloat16)
    grad_gate = contract_rows(inputs, gate_grad).astype(jnp.bfloat16)
    grad_up = contract_rows(inputs, up_grad).astype(jnp.bfloat16)
    grad_input = lax.psum_scatter(
        contract_cols(gate_grad, gate_weight) + contract_cols(up_grad, up_weight),
        ("out", "dep"),
        scatter_dimension=0,
        tiled=True,
    )
    return (grad_input.astype(jnp.bfloat16), grad_gate, grad_up, grad_down)


def solution(mesh):
    return jax.shard_map(
        on_device,
        mesh=mesh,
        in_specs=(
            P(("out", "dep"), "inp"),
            P(("out", "dep"), "inp"),
            P("inp", ("out", "dep")),
            P("inp", ("out", "dep")),
            P(("out", "dep"), "inp"),
            P(("out", "dep")),
            P(("out", "dep")),
            P(),
            P(),
        ),
        out_specs=(
            P(("out", "dep"), "inp"),
            P("inp", ("out", "dep")),
            P("inp", ("out", "dep")),
            P(("out", "dep"), "inp"),
        ),
        check_vma=False,
    )
```

profile of v0, /device:TPU:0, one launch (start us, length us, event | category | flops | bytes accessed | tf_op | source)
XLA Modules:
  0.0 487.4 jit_solution(3562528055836279850)
XLA Ops:
  7.2 0.0 all-gather.5.cloned.1.call-start
  7.2 0.7 all-gather.5.cloned.1.call-update
  7.9 0.0 all-gather.3.cloned.1.call-start
  7.9 0.7 convert_element_type.43
  8.6 0.9 select_reduce_fusion.1
  9.5 0.7 multiply_add_fusion
  10.1 0.2 select_reduce_fusion
  10.3 0.7 fusion.2
  11.0 1.6 multiply_convert_fusion.4
  12.5 0.0 all-gather.3.cloned.1.call-update
  12.6 0.0 all-reduce.3.cloned.1.call-start
  12.6 73.2 %all-gather.5.cloned.1.call-done = bf16[512,2048]{1,0:T(8,128)(2,1)} async-done(((bf16[16,2048]{1,0:T(8,128)(2,1)}), bf16[512,2048]{1,0:T(8,128)(2,1)}) %all-gather.5.cloned.1.call-update) | async-done | bytes 2097168 | tf_op jit(solution)/shard_map/all_gather | solution.py:56
  85.8 0.0 copy-start.1
  85.8 0.0 copy-start.4
  85.8 6.4 %fusion.5 = f32[512,896]{1,0:T(8,128)} fusion(bf16[512,2048]{1,0:T(8,128)(2,1)} %all-gather.5.cloned.1.call-done, bf16[2048,896]{1,0:T(8,128)(2,1)} %param.12), kind=kOutput, calls=%fused_computation.19 | convolution fusion | flops 1879048192 | bytes 7602176 | tf_op jit(solution)/shard_map/dot_general | solution.py:58
  92.2 0.0 copy-done.1
  92.2 0.0 copy-done.4
  92.2 3.6 fusion.6
  95.7 62.8 %all-gather.3.cloned.1.call-done = bf16[512,2048]{1,0:T(8,128)(2,1)} async-done(((bf16[16,2048]{1,0:T(8,128)(2,1)}), bf16[512,2048]{1,0:T(8,128)(2,1)}) %all-gather.3.cloned.1.call-update) | async-done | bytes 2097168 | tf_op jit(solution)/shard_map/all_gather | solution.py:61
  158.5 6.3 %fusion.4 = f32[512,896]{1,0:T(8,128)} fusion(bf16[512,2048]{1,0:T(8,128)(2,1)} %all-gather.3.cloned.1.call-done, bf16[896,2048]{1,0:T(8,128)(2,1)} %param.13), kind=kOutput, calls=%fused_computation.18 | convolution fusion | flops 1879048192 | bytes 7602176 | tf_op jit(solution)/shard_map/dot_general | solution.py:46
  164.8 0.0 all-reduce.3.cloned.1.call-update
  164.8 0.2 reduce-scatter.2.cloned.1.call-start
  165.1 110.0 %all-reduce.3.cloned.1.call-done = (f32[512,896]{1,0:T(8,128)}, f32[512,896]{1,0:T(8,128)}, f32[512,896]{1,0:T(8,128)}) async-done(((f32[512,896]{1,0:T(8,128)}, f32[512,896]{1,0:T(8,128)}, f32[512,896]{1,0:T(8,128)}), (f32[512,896]{1,0:T(8,128)}, f32[512,896]{1,0:T(8,128)}, f32[512,896]{1,0:T(8,128)})) %all-reduce.3.cloned.1.call-update) | async-done | bytes 5505040 | tf_op jit(solution)/shard_map/psum | solution.py:59
  275.1 0.0 copy-start.2
  275.1 3.6 multiply_convert_fusion.1
  278.7 0.1 copy-done.2
  278.7 0.0 copy-start.3
  278.7 2.4 fusion.7
  281.1 0.0 copy-done.3
  281.1 4.3 convolution_add_fusion
  285.4 0.0 reduce-scatter.2.cloned.1.call-update
  285.5 5.5 %convert_bitcast_fusion.1 = bf16[2048,896]{0,1:T(8,128)(2,1)} fusion(bf16[512,896]{1,0:T(8,128)(2,1)S(1)} %get-tuple-element.16, bf16[512,2048]{1,0:T(8,128)(2,1)} %all-gather.5.cloned.1.call-done), kind=kOutput, calls=%fused_computation.1 | convolution fusion | flops 1880883200 | bytes 6684672 | tf_op jit(solution)/shard_map/dot_general | solution.py:40
  291.0 0.0 copy-start.5
  291.0 6.3 %copy.15 = bf16[2048,896]{1,0:T(8,128)(2,1)} copy(bf16[2048,896]{0,1:T(8,128)(2,1)} %convert_bitcast_fusion.1) | data formatting | bytes 7340032
  297.3 0.0 copy-done.5
  297.3 3.9 convert_bitcast_fusion
  301.2 0.0 copy-start
  301.2 6.2 %copy.16 = bf16[2048,896]{1,0:T(8,128)(2,1)} copy(bf16[2048,896]{0,1:T(8,128)(2,1)} %convert_bitcast_fusion) | data formatting | bytes 7340032
  307.4 0.0 copy-done
  307.4 6.2 %convolution_convert_fusion = bf16[896,2048]{1,0:T(8,128)(2,1)} fusion(bf16[512,2048]{1,0:T(8,128)(2,1)} %all-gather.3.cloned.1.call-done, f32[512,896]{1,0:T(8,128)} %get-tuple-element.14, f32[512,896]{1,0:T(8,128)S(1)} %copy-done), kind=kOutput, calls=%fused_computation.2 | convolution fusion | flops 1883635712 | bytes 9437184 | tf_op jit(solution)/shard_map/dot_general | solution.py:40
  313.6 165.7 %reduce-scatter.2.cloned.1.call-done = f32[16,2048]{1,0:T(8,128)} async-done(((f32[512,2048]{1,0:T(8,128)}), f32[16,2048]{1,0:T(8,128)}) %reduce-scatter.2.cloned.1.call-update) | async-done | bytes 131088 | tf_op jit(solution)/shard_map/reduce_scatter | solution.py:68
  479.3 1.5 convert_element_type.47
Async XLA Ops:
  7.2 78.6 %all-gather.5.cloned.1.call-start = ((), (), s32[]{:S(2)}) async-start(), calls=%async_computation.2 | async-start | bytes 2162688 | tf_op jit(solution)/shard_map/all_gather | solution.py:56
  7.9 150.6 %all-gather.3.cloned.1.call-start = ((), (), s32[]{:S(2)}) async-start(), calls=%async_computation.1 | async-start | bytes 2162688 | tf_op jit(solution)/shard_map/all_gather | solution.py:61
  12.6 262.5 %all-reduce.3.cloned.1.call-start = ((), (), s32[]{:S(2)}) async-start(), calls=%async_computation.4 | async-start | bytes 11010048 | tf_op jit(solution)/shard_map/psum | solution.py:59
  85.8 6.4 %copy-start.1 = (bf16[2048,896]{1,0:T(8,128)(2,1)S(1)}, bf16[2048,896]{1,0:T(8,128)(2,1)}, u32[]{:S(2)}) copy-start(bf16[2048,896]{1,0:T(8,128)(2,1)} %param.11) | copy-start | bytes 11010052
  85.8 6.4 %copy-start.4 = (bf16[512,2048]{1,0:T(8,128)(2,1)S(1)}, bf16[512,2048]{1,0:T(8,128)(2,1)}, u32[]{:S(2)}) copy-start(bf16[512,2048]{1,0:T(8,128)(2,1)} %all-gather.5.cloned.1.call-done) | copy-start | bytes 6291460
  164.8 314.5 %reduce-scatter.2.cloned.1.call-start = ((), (), s32[]{:S(2)}) async-start(), calls=%async_computation.3 | async-start | bytes 4325376 | tf_op jit(solution)/shard_map/reduce_scatter | solution.py:68
  275.1 3.7 copy-start.2
  278.7 2.4 copy-start.3
  291.0 6.3 %copy-start.5 = (bf16[512,2048]{1,0:T(8,128)(2,1)S(1)}, bf16[512,2048]{1,0:T(8,128)(2,1)}, u32[]{:S(2)}) copy-start(bf16[512,2048]{1,0:T(8,128)(2,1)} %all-gather.5.cloned.1.call-done) | copy-start | bytes 6291460
  301.2 6.2 %copy-start = (f32[512,896]{1,0:T(8,128)S(1)}, f32[512,896]{1,0:T(8,128)}, u32[]{:S(2)}) copy-start(f32[512,896]{1,0:T(8,128)} %get-tuple-element.12) | copy-start | bytes 5505028
Sparse Core Ops, SparseCore 0:
  11.0 74.7 all-gather.4
  89.3 69.1 all-gather.2
  164.9 110.0 all-reduce.2
  285.6 193.6 reduce-scatter.1
where the time goes:
time: 488 us; the launch traced here: 487 us
  waiting for transfers between devices  412 us (84%)
  matrix products  38.5 us (8%)
  between operations  13.8 us (3%)
  local copies, waits for them, and re-layouts  12.6 us (3%)
  other arithmetic  9.74 us (2%)
    reduce_scatter x1, waiting for transfers between devices, on_device(): lax.psum_scatter(contract_cols(gate_grad, gate_weight) + contract_cols(up...  166 us
    psum x1, waiting for transfers between devices, on_device(): gate_sum, up_sum = lax.psum((gate_part, up_part), 'inp')  110 us
    all_gather x1, waiting for transfers between devices, on_device(): inputs = lax.all_gather(tokens, ('out', 'dep'), axis=0, tiled=True)  73.2 us
    all_gather x1, waiting for transfers between devices, on_device(): out_grad = lax.all_gather(local_grad, ('out', 'dep'), axis=0, tiled=True)  62.8 us
    dot_general x3, matrix products, contract_rows(): lax.dot_general(left, right, (((0,), (0,)), ((), ())), preferred_element_...  15.6 us
    dot_general x3, matrix products, contract_cols(): lax.dot_general(left, right, (((1,), (1,)), ((), ())), preferred_element_...  12.9 us
    unnamed x14, local copies, waits for them, and re-layouts  12.6 us
  transfers between devices with their start and end apart: 4, of which 4 were waited for; matrix products, arithmetic and copies ran while one was open for 9% of the time, Pallas kernels for 0%

commit v1 on v0

v1 whole, which is shorter than its diff:
```python
import jax
import jax.numpy as jnp
from jax import lax
from jax.experimental import pallas as pl
from jax.experimental.pallas import tpu as pltpu
from jax.sharding import PartitionSpec as P

SIMPO_BETA = 2.5
LOSS_SCALE = 64.0
MESH = pl.DeviceIdType.MESH
BF16 = jnp.bfloat16
F32 = jnp.float32

WIDTH = 2048
HALF = 1024
UNITS = 896
ROWS = 16
CHUNK = 256
OWN = 128


def dot(left, right, dims):
    return lax.dot_general(left, right, (dims, ((), ())), preferred_element_type=F32)


def kernel(
    tok_ref,
    cot_ref,
    gate_ref,
    up_ref,
    down_ref,
    seq_ref,
    chosen_ref,
    margin_ref,
    count_ref,
    gin_ref,
    ggate_ref,
    gup_ref,
    gdown_ref,
    wgu,
    wdn,
    tok,
    og,
    ogown,
    part,
    xs,
    xr,
    summed,
    zs,
    zr,
    hid,
    gug,
    gpart,
    ra1,
    rb1,
    sa,
    sb,
    r2,
    fin,
    hsrc,
    hdst,
    wsem,
    hsem_s,
    hsem_r,
    ag_s,
    ag_r,
    x_s,
    x_r,
    z_s,
    z_r,
    c_s,
    c_r,
    rs_s,
    rs_r,
    f_s,
    f_r,
):
    inp, x, dep = lax.axis_index("inp"), lax.axis_index("out"), lax.axis_index("dep")
    zl, core = inp // 2, inp % 2
    y, zh = dep // 2, dep % 2
    at_x = lambda d: (inp, (x + d) % 4, dep)
    at_y = lambda d: (inp, x, ((y + d) % 4) * 2 + zh)
    at_zh = (inp, x, y * 2 + 1 - zh)
    at_core = (zl * 2 + 1 - core, x, dep)
    at_zl = ((1 - zl) * 2 + core, x, dep)

    loads = [
        pltpu.make_async_copy(gate_ref, wgu.at[:, pl.ds(0, UNITS)], wsem.at[0]),
        pltpu.make_async_copy(up_ref, wgu.at[:, pl.ds(UNITS, UNITS)], wsem.at[1]),
        pltpu.make_async_copy(down_ref, wdn, wsem.at[2]),
    ]
    for cp in loads:
        cp.start()

    barrier = pltpu.get_barrier_semaphore()
    greeted = [at_x(1), at_x(2), at_x(3), at_y(1), at_y(2), at_y(3), at_zh, at_core, at_zl]
    for who in greeted:
        pl.semaphore_signal(barrier, inc=1, device_id=who, device_id_type=MESH)

    sent = []

    def send(src, dst, s_sem, r_sem, who):
        cp = pltpu.make_async_remote_copy(
            src_ref=src, dst_ref=dst, send_sem=s_sem, recv_sem=r_sem, device_id=who, device_id_type=MESH
        )
        cp.start()
        sent.append(cp)
        return cp

    tok[0, x, y] = tok_ref[...]
    row = lax.broadcasted_iota(jnp.int32, (ROWS, 128), 0)
    margin = jnp.zeros((ROWS, 128), F32)
    length = jnp.ones((ROWS, 128), F32)
    polarity = jnp.zeros((ROWS, 128), F32)
    for t in range(ROWS):
        pair, pick = seq_ref[t], chosen_ref[t]
        margin = jnp.where(row == t, margin_ref[pair], margin)
        length = jnp.where(row == t, count_ref[2 * pair + pick].astype(F32), length)
        polarity = jnp.where(row == t, 1.0 - 2.0 * pick.astype(F32), polarity)
    weight = polarity * SIMPO_BETA * LOSS_SCALE * jax.nn.sigmoid(-margin) / length
    for j in range(WIDTH // 128):
        cols = pl.ds(j * 128, 128)
        value = (cot_ref[:, cols].astype(F32) * weight).astype(BF16)
        ogown[:, cols] = value
        og[0, x, y, :, cols] = value

    pl.semaphore_wait(barrier, len(greeted))

    bufs = (tok, og)
    cols_of = (pl.ds(0, HALF), pl.ds(HALF, HALF))

    def ag1(a, s):
        got = []
        for h in range(2):
            for d in range(1, 4):
                spot = bufs[a].at[s, x, y, :, cols_of[h]]
                who = at_y(d) if h == 0 else at_x(d)
                got.append(send(spot, spot, ag_s.at[a, s, h, 0, d - 1], ag_r.at[a, s, h, 0, d - 1], who))
        return got

    def ag2(a, s):
        got = []
        for h in range(2):
            for d in range(1, 4):
                if h == 0:
                    spot, who = bufs[a].at[s, x, :, :, cols_of[h]], at_x(d)
                else:
                    spot, who = bufs[a].at[s, :, y, :, cols_of[h]], at_y(d)
                got.append(send(spot, spot, ag_s.at[a, s, h, 1, d - 1], ag_r.at[a, s, h, 1, d - 1], who))
        return got

    def arrived(cps):
        for cp in cps:
            cp.wait_recv()

    t01 = ag1(0, 0)
    hops = [
        send(tok_ref, tok.at[1, x, y], hsem_s.at[0], hsem_r.at[0], at_zh),
        send(ogown, og.at[1, x, y], hsem_s.at[1], hsem_r.at[1], at_zh),
    ]
    o01 = ag1(1, 0)
    arrived(t01)
    t02 = ag2(0, 0)
    arrived(hops)
    t11 = ag1(0, 1)
    o11 = ag1(1, 1)
    arrived(o01)

    mine = pl.ds(pl.multiple_of(core * OWN, OWN), OWN)
    other = pl.ds(pl.multiple_of((1 - core) * OWN, OWN), OWN)

    def piece_cols(p):
        return pl.ds(p * UNITS, UNITS)

    def multiply(s, p):
        if p < 2:
            part[p] = dot(tok[s].reshape(CHUNK, WIDTH), wgu[:, piece_cols(p)], ((1,), (0,)))
        else:
            part[p] = dot(og[s].reshape(CHUNK, WIDTH), wdn[...], ((1,), (1,)))
        xs[s, p] = part[p, other].astype(BF16)
        return send(xs.at[s, p], xr.at[s, p], x_s.at[s, p], x_r.at[s, p], at_core)

    def pair_sum(s, p, cp):
        cp.wait_recv()
        total = part[p, mine] + xr[s, p].astype(F32)
        summed[s, p] = total
        zs[s, p] = total.astype(BF16)
        return send(zs.at[s, p], zr.at[s, p], z_s.at[s, p], z_r.at[s, p], at_zl)

    zcp = {}

    def gate_up(s):
        first = multiply(s, 0)
        second = multiply(s, 1)
        zcp[s, 0] = pair_sum(s, 0, first)
        zcp[s, 1] = pair_sum(s, 1, second)

    def hidden_grad(s):
        third = multiply(s, 2)
        zcp[s, 2] = pair_sum(s, 2, third)

    loads[0].wait()
    loads[1].wait()
    arrived(t02)
    o02 = ag2(1, 0)
    gate_up(0)
    arrived(t11)
    arrived(o02)
    t12 = ag2(0, 1)
    loads[2].wait()
    hidden_grad(0)
    arrived(o11)
    arrived(t12)
    o12 = ag2(1, 1)
    gate_up(1)
    arrived(o12)
    hidden_grad(1)

    def activate(s):
        for p in range(3):
            zcp[s, p].wait_recv()

        def rows16(i, carry):
            rows = pl.ds(pl.multiple_of(i * 16, 16), 16)
            gate_sum = summed[s, 0, rows] + zr[s, 0, rows].astype(F32)
            up_sum = summed[s, 1, rows] + zr[s, 1, rows].astype(F32)
            hg = summed[s, 2, rows] + zr[s, 2, rows].astype(F32)
            logistic = jax.nn.sigmoid(gate_sum)
            swish = gate_sum * logistic
            at = pl.ds(pl.multiple_of(core * OWN + i * 16, 16), 16)
            gug[s, at, pl.ds(0, UNITS)] = (
                hg * up_sum * logistic * (1.0 + gate_sum * (1.0 - logistic))
            ).astype(BF16)
            gug[s, at, pl.ds(UNITS, UNITS)] = (hg * swish).astype(BF16)
            hid[s, at] = (swish * up_sum).astype(BF16)
            return carry

        lax.fori_loop(0, OWN // 16, rows16, 0)
        return [
            send(gug.at[s, mine], gug.at[s, mine], c_s.at[s, 0], c_r.at[s, 0], at_core),
            send(hid.at[s, mine], hid.at[s, mine], c_s.at[s, 1], c_r.at[s, 1], at_core),
        ]

    def grad_in(s):
        got = []
        for h in range(2):
            for q in range(2):
                cols = pl.ds(h * HALF + q * 512, 512)
                value = dot(gug[s], wgu[cols, :], ((1,), (1,))).astype(BF16)
                gpart[s, :, :, :, cols] = value.reshape(4, 4, ROWS, 512)
            for d in range(1, 4):
                if h == 0:
                    src, dst, who = gpart.at[s, (x + d) % 4, :, :, cols_of[0]], ra1.at[s, d - 1], at_x(d)
                else:
                    src, dst, who = gpart.at[s, :, (y + d) % 4, :, cols_of[1]], rb1.at[s, d - 1], at_y(d)
                got.append(send(src, dst, rs_s.at[s, h, 0, d - 1], rs_r.at[s, h, 0, d - 1], who))
        return got

    def scatter2(s, cps):
        arrived(cps)
        got = []
        total = gpart[s, x, :, :, cols_of[0]].astype(F32)
        for d in range(3):
            total += ra1[s, d].astype(F32)
        sa[s] = total.astype(BF16)
        total = gpart[s, :, y, :, cols_of[1]].astype(F32)
        for d in range(3):
            total += rb1[s, d].astype(F32)
        sb[s] = total.astype(BF16)
        for d in range(1, 4):
            got.append(
                send(sa.at[s, (y + d) % 4], r2.at[s, 0, d - 1], rs_s.at[s, 0, 1, d - 1], rs_r.at[s, 0, 1, d - 1], at_y(d))
            )
            got.append(
                send(sb.at[s, (x + d) % 4], r2.at[s, 1, d - 1], rs_s.at[s, 1, 1, d - 1], rs_r.at[s, 1, 1, d - 1], at_x(d))
            )
        return got

    def scatter_sum(s, cps):
        arrived(cps)
        a, b = sa[s, y].astype(F32), sb[s, x].astype(F32)
        for d in range(3):
            a += r2[s, 0, d].astype(F32)
            b += r2[s, 1, d].astype(F32)
        return a, b

    ccp = activate(0)
    arrived(ccp)
    g0 = grad_in(0)
    p0 = scatter2(0, g0)
    ccp = activate(1)
    arrived(ccp)
    g1 = grad_in(1)
    a, b = scatter_sum(0, p0)
    fin[:, cols_of[0]] = a
    fin[:, cols_of[1]] = b

    def gate_tile(i, carry):
        rows = pl.ds(pl.multiple_of(i * 256, 256), 256)
        left = tok[:, :, :, :, rows].reshape(2 * CHUNK, 256)
        value = dot(left, gug[...].reshape(2 * CHUNK, 2 * UNITS), ((0,), (0,)))
        ggate_ref[rows, :] = value[:, :UNITS].astype(BF16)
        gup_ref[rows, :] = value[:, UNITS:].astype(BF16)
        return carry

    lax.fori_loop(0, WIDTH // 256, gate_tile, 0)
    p1 = scatter2(1, g1)

    def down_tile(i, carry):
        rows = pl.ds(pl.multiple_of(i * 128, 128), 128)
        left = hid[:, :, rows].reshape(2 * CHUNK, 128)
        value = dot(left, og[...].reshape(2 * CHUNK, WIDTH), ((0,), (0,)))
        gdown_ref[rows, :] = value.astype(BF16)
        return carry

    lax.fori_loop(0, UNITS // 128, down_tile, 0)
    a, b = scatter_sum(1, p1)
    hsrc[:, cols_of[0]] = a.astype(BF16)
    hsrc[:, cols_of[1]] = b.astype(BF16)
    last = send(hsrc, hdst, f_s.at[0], f_r.at[0], at_zh)
    last.wait_recv()
    gin_ref[...] = (fin[...] + hdst[...].astype(F32)).astype(BF16)
    for cp in sent:
        cp.wait_send()


def on_device(tokens, cotangent, gate_weight, up_weight, down_weight, seq_ids, chosen, margins, counts):
    vmem = pl.BlockSpec(memory_space=pltpu.VMEM)
    smem = pl.BlockSpec(memory_space=pltpu.SMEM)
    hbm = pl.BlockSpec(memory_space=pl.ANY)
    dma = pltpu.SemaphoreType.DMA
    return pl.pallas_call(
        kernel,
        out_shape=(
            jax.ShapeDtypeStruct((ROWS, WIDTH), BF16),
            jax.ShapeDtypeStruct((WIDTH, UNITS), BF16),
            jax.ShapeDtypeStruct((WIDTH, UNITS), BF16),
            jax.ShapeDtypeStruct((UNITS, WIDTH), BF16),
        ),
        in_specs=[vmem, vmem, hbm, hbm, hbm, smem, smem, smem, smem],
        out_specs=(vmem, vmem, vmem, vmem),
        scratch_shapes=[
            pltpu.VMEM((WIDTH, 2 * UNITS), BF16),
            pltpu.VMEM((UNITS, WIDTH), BF16),
            pltpu.VMEM((2, 4, 4, ROWS, WIDTH), BF16),
            pltpu.VMEM((2, 4, 4, ROWS, WIDTH), BF16),
            pltpu.VMEM((ROWS, WIDTH), BF16),
            pltpu.VMEM((3, CHUNK, UNITS), F32),
            pltpu.VMEM((2, 3, OWN, UNITS), BF16),
            pltpu.VMEM((2, 3, OWN, UNITS), BF16),
            pltpu.VMEM((2, 3, OWN, UNITS), F32),
            pltpu.VMEM((2, 3, OWN, UNITS), BF16),
            pltpu.VMEM((2, 3, OWN, UNITS), BF16),
            pltpu.VMEM((2, CHUNK, UNITS), BF16),
            pltpu.VMEM((2, CHUNK, 2 * UNITS), BF16),
            pltpu.VMEM((2, 4, 4, ROWS, WIDTH), BF16),
            pltpu.VMEM((2, 3, 4, ROWS, HALF), BF16),
            pltpu.VMEM((2, 3, 4, ROWS, HALF), BF16),
            pltpu.VMEM((2, 4, ROWS, HALF), BF16),
            pltpu.VMEM((2, 4, ROWS, HALF), BF16),
            pltpu.VMEM((2, 2, 3, ROWS, HALF), BF16),
            pltpu.VMEM((ROWS, WIDTH), F32),
            pltpu.VMEM((ROWS, WIDTH), BF16),
            pltpu.VMEM((ROWS, WIDTH), BF16),
            dma((3,)),
            dma((2,)),
            dma((2,)),
            dma((2, 2, 2, 2, 3)),
            dma((2, 2, 2, 2, 3)),
            dma((2, 3)),
            dma((2, 3)),
            dma((2, 3)),
            dma((2, 3)),
            dma((2, 2)),
            dma((2, 2)),
            dma((2, 2, 2, 3)),
            dma((2, 2, 2, 3)),
            dma((1,)),
            dma((1,)),
        ],
        compiler_params=pltpu.CompilerParams(
            collective_id=0, has_side_effects=True, vmem_limit_bytes=60 << 20
        ),
        cost_estimate=pl.CostEstimate(flops=15_000_000_000, bytes_accessed=22_000_000, transcendentals=0),
        name="simpo_backward",
    )(tokens, cotangent, gate_weight, up_weight, down_weight, seq_ids, chosen, margins, counts)


def solution(mesh):
    return jax.shard_map(
        on_device,
        mesh=mesh,
        in_specs=(
            P(("out", "dep"), "inp"),
            P(("out", "dep"), "inp"),
            P("inp", ("out", "dep")),
            P("inp", ("out", "dep")),
            P(("out", "dep"), "inp"),
            P(("out", "dep")),
            P(("out", "dep")),
            P(),
            P(),
        ),
        out_specs=(
            P(("out", "dep"), "inp"),
            P("inp", ("out", "dep")),
            P("inp", ("out", "dep")),
            P(("out", "dep"), "inp"),
        ),
        check_vma=False,
    )
```

time: 488 us -> 95.1 us (0.19)
  waiting for transfers between devices: 412 us -> 0 us
  Pallas kernels: 0 us -> 82.7 us
  matrix products: 38.5 us -> 0 us
  between operations: 13.8 us -> 0.65 us
  other arithmetic: 9.74 us -> 0 us
    reduce_scatter x1 -> x0, waiting for transfers between devices: 166 us -> none  [on_device(): lax.psum_scatter(contract_cols(gate_grad, gate_weight) + contract_cols(up...]
    all_gather x2 -> x0, waiting for transfers between devices: 136 us -> none  [the longest x1 73.2 us: on_device(): inputs = lax.all_gather(tokens, ('out', 'dep'), axis=0, tiled=True)]
    psum x1 -> x0, waiting for transfers between devices: 110 us -> none  [on_device(): gate_sum, up_sum = lax.psum((gate_part, up_part), 'inp')]
    pallas_call x0 -> x1, Pallas kernels: none -> 82.7 us  [on_device(): pl.pallas_call(kernel, out_shape=(jax.ShapeDtypeStruct((ROWS, WIDTH), BF1...]
    dot_general x8 -> x0, matrix products: 38.5 us -> none  [the longest x3 15.6 us: contract_rows(): lax.dot_general(left, right, (((0,), (0,)), ((), ())), preferred_element_...]
    convert_element_type x4 -> x0, other arithmetic: 7.36 us -> none  [the longest x1 3.61 us: act_grads(): up_grad = (hidden_grad * swish).astype(jnp.bfloat16)]
    unnamed x14 -> x8, local copies, waits for them, and re-layouts: 12.6 us -> 11 us
  transfers between devices with their start and end apart: 4 -> 0, of which waited for: 4 -> 0; matrix products, arithmetic and copies ran while one was open for 9% -> 0% of each run, Pallas kernels for 0% -> 0%
where the time goes in v1:
time: 95.1 us; the launch traced here: 94.4 us
  Pallas kernels  82.7 us (87%)
  local copies, waits for them, and re-layouts  11 us (12%)
    pallas_call x1, Pallas kernels, on_device(): pl.pallas_call(kernel, out_shape=(jax.ShapeDtypeStruct((ROWS, WIDTH), BF1...  82.7 us
    unnamed x8, local copies, waits for them, and re-layouts  11 us

profile of v1, /device:TPU:0, one launch (start us, length us, event | category | flops | bytes accessed | tf_op | source)
XLA Modules:
  0.0 94.4 jit_solution(6400203145809632506)
XLA Ops:
  0.6 82.7 %simpo_backward.1 = (bf16[16,2048]{1,0:T(8,128)(2,1)}, bf16[2048,896]{1,0:T(8,128)(2,1)}, bf16[2048,896]{1,0:T(8,128)(2,1)}, bf16[896,2048]{1,0:T(8,128)(2,1)}) custom-call(bf16[16,2048]{1,0:T(8,128)(2,1)} %tok_ref.1, bf16[16,2048]{1,0:T(8,128)(2,1)} %cot_ref.1, bf16[2048,896]{1,0:T(8,128)(2,1)} %gate_ref.1, bf16[2048,896]{1,0:T(8,128)(2,1)} %up_ref.1, ...), custom_call_target="tpu_custom_call" | custom-call | flops 15000000512 | bytes 22000000 | tf_op jit(solution)/shard_map/simpo_backward/pallas_call | solution.py:332
  83.4 1.5 %copy.17 = bf16[16,2048]{1,0:T(8,128)(2,1)} copy(bf16[16,2048]{1,0:T(8,128)(2,1)} %get-tuple-element.8) | data formatting | bytes 131072
  84.9 0.0 copy-start.1
  84.9 4.3 %copy.18 = bf16[2048,896]{1,0:T(8,128)(2,1)} copy(bf16[2048,896]{1,0:T(8,128)(2,1)} %get-tuple-element.9) | data formatting | bytes 7340032
  89.2 0.0 copy-done.1
  89.2 0.0 copy-start
  89.2 1.9 %copy.19 = bf16[2048,896]{1,0:T(8,128)(2,1)} copy(bf16[2048,896]{1,0:T(8,128)(2,1)S(1)} %copy-done.1) | data formatting | bytes 7340032
  91.0 1.5 %copy-done = bf16[896,2048]{1,0:T(8,128)(2,1)S(1)} copy-done((bf16[896,2048]{1,0:T(8,128)(2,1)S(1)}, bf16[896,2048]{1,0:T(8,128)(2,1)}, u32[]{:S(2)}) %copy-start) | copy-done | bytes 3670040
  92.5 1.8 %copy.20 = bf16[896,2048]{1,0:T(8,128)(2,1)} copy(bf16[896,2048]{1,0:T(8,128)(2,1)S(1)} %copy-done) | data formatting | bytes 7340032
Async XLA Ops:
  84.9 4.3 %copy-start.1 = (bf16[2048,896]{1,0:T(8,128)(2,1)S(1)}, bf16[2048,896]{1,0:T(8,128)(2,1)}, u32[]{:S(2)}) copy-start(bf16[2048,896]{1,0:T(8,128)(2,1)} %get-tuple-element.10) | copy-start | bytes 11010052
  89.2 3.4 %copy-start = (bf16[896,2048]{1,0:T(8,128)(2,1)S(1)}, bf16[896,2048]{1,0:T(8,128)(2,1)}, u32[]{:S(2)}) copy-start(bf16[896,2048]{1,0:T(8,128)(2,1)} %get-tuple-element.11) | copy-start | bytes 11010052

commit v2 on v1

v2 whole, which is shorter than its diff:
```python
import jax
import jax.numpy as jnp
from jax import lax
from jax.experimental import pallas as pl
from jax.experimental.pallas import tpu as pltpu
from jax.sharding import PartitionSpec as P

SIMPO_BETA = 2.5
LOSS_SCALE = 64.0
MESH = pl.DeviceIdType.MESH
BF16 = jnp.bfloat16
F32 = jnp.float32

WIDTH = 2048
HALF = 1024
UNITS = 896
ROWS = 16
CHUNK = 256
OWN = 128
PIECES = (((0, 512), (512, 384)), ((0, UNITS),))


def dot(left, right, dims):
    return lax.dot_general(left, right, (dims, ((), ())), preferred_element_type=F32)


def kernel(
    tok_ref,
    cot_ref,
    gate_ref,
    up_ref,
    down_ref,
    seq_ref,
    chosen_ref,
    margin_ref,
    count_ref,
    gin_ref,
    ggate_ref,
    gup_ref,
    gdown_ref,
    wgate,
    wup,
    wdn,
    tok,
    og,
    cot,
    ogown,
    part,
    xs,
    xr,
    summed,
    zs,
    zr,
    slope,
    swished,
    hid,
    gug,
    gacc,
    gpart,
    ra1,
    rb1,
    sa,
    sb,
    r2,
    sa1,
    sb1,
    r21,
    fin,
    hsrc,
    hdst,
    lsem,
    hsem_s,
    hsem_r,
    ag_s,
    ag_r,
    x_s,
    x_r,
    z_s,
    z_r,
    c_s,
    c_r,
    k_s,
    k_r,
    rs_s,
    rs_r,
    f_s,
    f_r,
):
    inp, x, dep = lax.axis_index("inp"), lax.axis_index("out"), lax.axis_index("dep")
    zl, core = inp // 2, inp % 2
    y, zh = dep // 2, dep % 2
    at_x = lambda d: (inp, (x + d) % 4, dep)
    at_y = lambda d: (inp, x, ((y + d) % 4) * 2 + zh)
    at_zh = (inp, x, y * 2 + 1 - zh)
    at_core = (zl * 2 + 1 - core, x, dep)
    at_zl = ((1 - zl) * 2 + core, x, dep)

    barrier = pltpu.get_barrier_semaphore()
    greeted = [at_x(1), at_x(2), at_x(3), at_y(1), at_y(2), at_y(3), at_zh, at_core, at_zl]
    for who in greeted:
        pl.semaphore_signal(barrier, inc=1, device_id=who, device_id_type=MESH)

    def load(src, dst, i):
        cp = pltpu.make_async_copy(src, dst, lsem.at[i])
        cp.start()
        return cp

    cot_load = load(cot_ref, cot, 0)
    tok_load = load(tok_ref, tok.at[0, x, y], 1)
    gate_load = load(gate_ref, wgate, 2)
    up_load = load(up_ref, wup, 3)
    down_load = load(down_ref, wdn, 4)

    sent = []

    def send(src, dst, s_sem, r_sem, who):
        cp = pltpu.make_async_remote_copy(
            src_ref=src, dst_ref=dst, send_sem=s_sem, recv_sem=r_sem, device_id=who, device_id_type=MESH
        )
        cp.start()
        sent.append(cp)
        return cp

    def arrived(cps):
        for cp in cps:
            cp.wait_recv()

    bufs = (tok, og)
    cols_of = (pl.ds(0, HALF), pl.ds(HALF, HALF))

    def ag1(a, s, own=None):
        got = []
        for d in range(1, 4):
            for h in range(2):
                spot = bufs[a].at[s, x, y, :, cols_of[h]]
                src = spot if own is None else own.at[:, cols_of[h]]
                who = at_y(d) if h == 0 else at_x(d)
                got.append(send(src, spot, ag_s.at[a, s, h, 0, d - 1], ag_r.at[a, s, h, 0, d - 1], who))
        return got

    def ag2(a, s):
        got = []
        for d in range(1, 4):
            for h in range(2):
                if h == 0:
                    spot, who = bufs[a].at[s, x, :, :, cols_of[h]], at_x(d)
                else:
                    spot, who = bufs[a].at[s, :, y, :, cols_of[h]], at_y(d)
                got.append(send(spot, spot, ag_s.at[a, s, h, 1, d - 1], ag_r.at[a, s, h, 1, d - 1], who))
        return got

    pl.semaphore_wait(barrier, len(greeted))
    t01 = ag1(0, 0, tok_ref)
    tok_hop = send(tok_ref, tok.at[1, x, y], hsem_s.at[0], hsem_r.at[0], at_zh)

    row = lax.broadcasted_iota(jnp.int32, (ROWS, 128), 0)
    margin = jnp.zeros((ROWS, 128), F32)
    length = jnp.ones((ROWS, 128), F32)
    polarity = jnp.zeros((ROWS, 128), F32)
    for t in range(ROWS):
        pair, pick = seq_ref[t], chosen_ref[t]
        margin = jnp.where(row == t, margin_ref[pair], margin)
        length = jnp.where(row == t, count_ref[2 * pair + pick].astype(F32), length)
        polarity = jnp.where(row == t, 1.0 - 2.0 * pick.astype(F32), polarity)
    weight = polarity * SIMPO_BETA * LOSS_SCALE * jax.nn.sigmoid(-margin) / length
    cot_load.wait()
    for j in range(WIDTH // 128):
        cols = pl.ds(j * 128, 128)
        value = (cot[:, cols].astype(F32) * weight).astype(BF16)
        ogown[:, cols] = value
        og[0, x, y, :, cols] = value
    og_hop = send(ogown, og.at[1, x, y], hsem_s.at[1], hsem_r.at[1], at_zh)

    tok_load.wait()
    arrived(t01)
    t02 = ag2(0, 0)
    arrived([tok_hop])
    t11 = ag1(0, 1)

    mine = pl.ds(pl.multiple_of(core * OWN, OWN), OWN)
    other = pl.ds(pl.multiple_of((1 - core) * OWN, OWN), OWN)

    def multiply(s, p):
        if p == 0:
            part[p] = dot(tok[s].reshape(CHUNK, WIDTH), wgate[...], ((1,), (0,)))
        elif p == 1:
            part[p] = dot(tok[s].reshape(CHUNK, WIDTH), wup[...], ((1,), (0,)))
        else:
            part[p] = dot(og[s].reshape(CHUNK, WIDTH), wdn[...], ((1,), (1,)))
        xs[s, p] = part[p, other].astype(BF16)
        return send(xs.at[s, p], xr.at[s, p], x_s.at[s, p], x_r.at[s, p], at_core)

    zcp = {}

    def pair_sum(s, p, cp, pieces=((0, UNITS),)):
        cp.wait_recv()
        total = part[p, mine] + xr[s, p].astype(F32)
        summed[s, p] = total
        zs[s, p] = total.astype(BF16)
        for k, (first, count) in enumerate(pieces):
            cols = pl.ds(first, count)
            zcp[s, p, k] = send(
                zs.at[s, p, :, cols], zr.at[s, p, :, cols], z_s.at[s, p, k], z_r.at[s, p, k], at_zl
            )

    def gate_up(s):
        first = multiply(s, 0)
        second = multiply(s, 1)
        pair_sum(s, 0, first)
        pair_sum(s, 1, second)

    def hidden_grad(s):
        pair_sum(s, 2, multiply(s, 2), PIECES[s])

    def by_rows(body):
        lax.fori_loop(0, OWN // 16, lambda i, c: (body(pl.multiple_of(i * 16, 16)), c)[1], 0)

    def activate(s):
        zcp[s, 0, 0].wait_recv()
        zcp[s, 1, 0].wait_recv()

        def body(i):
            rows = pl.ds(i, 16)
            gate_sum = summed[s, 0, rows] + zr[s, 0, rows].astype(F32)
            up_sum = summed[s, 1, rows] + zr[s, 1, rows].astype(F32)
            logistic = jax.nn.sigmoid(gate_sum)
            swish = gate_sum * logistic
            slope[s, rows] = up_sum * logistic * (1.0 + gate_sum * (1.0 - logistic))
            swished[s, rows] = swish
            hid[s, pl.ds(pl.multiple_of(core * OWN + i, 16), 16)] = (swish * up_sum).astype(BF16)

        by_rows(body)
        return send(hid.at[s, mine], hid.at[s, mine], c_s.at[s], c_r.at[s], at_core)

    def act_grad(s, k):
        zcp[s, 2, k].wait_recv()
        cols = pl.ds(*PIECES[s][k])

        def body(i):
            rows = pl.ds(i, 16)
            at = pl.ds(pl.multiple_of(core * OWN + i, 16), 16)
            hg = summed[s, 2, rows, cols] + zr[s, 2, rows, cols].astype(F32)
            gug[s, 0, at, cols] = (hg * slope[s, rows, cols]).astype(BF16)
            gug[s, 1, at, cols] = (hg * swished[s, rows, cols]).astype(BF16)

        by_rows(body)
        spot = gug.at[s, :, mine, cols]
        return send(spot, spot, k_s.at[s, k], k_r.at[s, k], at_core)

    def grad_in(s, ccps):
        got = []
        last = len(ccps) - 1
        for k, cp in enumerate(ccps):
            cp.wait_recv()
            cols = pl.ds(*PIECES[s][k])
            for h in range(2):
                for q in range(2):
                    wide = pl.ds(h * HALF + q * 512, 512)
                    value = dot(gug[s, 0, :, cols], wgate[wide, cols], ((1,), (1,)))
                    value += dot(gug[s, 1, :, cols], wup[wide, cols], ((1,), (1,)))
                    if k > 0:
                        value += gacc[:, wide]
                    if k < last:
                        gacc[:, wide] = value
                    else:
                        gpart[s, :, :, :, wide] = value.astype(BF16).reshape(4, 4, ROWS, 512)
                if k < last:
                    continue
                for d in range(1, 4):
                    if h == 0:
                        src, dst, who = gpart.at[s, (x + d) % 4, :, :, cols_of[0]], ra1.at[s, d - 1], at_x(d)
                    else:
                        src, dst, who = gpart.at[s, :, (y + d) % 4, :, cols_of[1]], rb1.at[s, d - 1], at_y(d)
                    got.append(send(src, dst, rs_s.at[s, h, 0, d - 1], rs_r.at[s, h, 0, d - 1], who))
        return got

    def scatter2(s, cps):
        arrived(cps)
        at_a, at_b, to, kind = ((sa, sb, r2, BF16), (sa1, sb1, r21, F32))[s]
        total = gpart[s, x, :, :, cols_of[0]].astype(F32)
        for d in range(3):
            total += ra1[s, d].astype(F32)
        at_a[...] = total.astype(kind)
        total = gpart[s, :, y, :, cols_of[1]].astype(F32)
        for d in range(3):
            total += rb1[s, d].astype(F32)
        at_b[...] = total.astype(kind)
        got = []
        for d in range(1, 4):
            got.append(
                send(at_a.at[(y + d) % 4], to.at[0, d - 1], rs_s.at[s, 0, 1, d - 1], rs_r.at[s, 0, 1, d - 1], at_y(d))
            )
            got.append(
                send(at_b.at[(x + d) % 4], to.at[1, d - 1], rs_s.at[s, 1, 1, d - 1], rs_r.at[s, 1, 1, d - 1], at_x(d))
            )
        return got

    def scatter_sum(s, cps, out):
        arrived(cps)
        at_a, at_b, to = ((sa, sb, r2), (sa1, sb1, r21))[s]
        for h, own in enumerate((at_a[y], at_b[x])):
            total = own.astype(F32)
            for d in range(3):
                total += to[h, d].astype(F32)
            out[:, cols_of[h]] = total

    arrived(t02)
    arrived(t11)
    t12 = ag2(0, 1)
    arrived([og_hop])
    o11 = ag1(1, 1)
    o01 = ag1(1, 0, ogown)
    gate_load.wait()
    up_load.wait()
    gate_up(0)
    arrived(t12)
    arrived(o11)
    o12 = ag2(1, 1)
    gate_up(1)
    arrived(o12)
    arrived(o01)
    o02 = ag2(1, 0)
    down_load.wait()
    hidden_grad(1)
    hid0 = activate(0)
    arrived(o02)
    hidden_grad(0)
    hid1 = activate(1)
    arrived([hid0, hid1])

    def down_tile(i, carry):
        rows = pl.ds(pl.multiple_of(i * 128, 128), 128)
        left = hid[:, :, rows].reshape(2 * CHUNK, 128)
        value = dot(left, og[...].reshape(2 * CHUNK, WIDTH), ((0,), (0,)))
        gdown_ref[rows, :] = value.astype(BF16)
        return carry

    lax.fori_loop(0, UNITS // 128, down_tile, 0)
    cc1 = [act_grad(1, k) for k in range(len(PIECES[1]))]
    g1 = grad_in(1, cc1)
    cc0 = [act_grad(0, k) for k in range(len(PIECES[0]))]
    g0 = grad_in(0, cc0)

    def gate_tile(i, carry):
        rows = pl.ds(pl.multiple_of(i * 256, 256), 256)
        left = tok[:, :, :, :, rows].reshape(2 * CHUNK, 256)
        right = jnp.concatenate(
            [gug[:, 0].reshape(2 * CHUNK, UNITS), gug[:, 1].reshape(2 * CHUNK, UNITS)], axis=1
        )
        value = dot(left, right, ((0,), (0,)))
        ggate_ref[rows, :] = value[:, :UNITS].astype(BF16)
        gup_ref[rows, :] = value[:, UNITS:].astype(BF16)
        return carry

    lax.fori_loop(0, 4, gate_tile, 0)
    p1 = scatter2(1, g1)
    lax.fori_loop(4, 8, gate_tile, 0)
    scatter_sum(1, p1, hsrc)
    last = send(hsrc, hdst, f_s.at[0], f_r.at[0], at_zh)
    p0 = scatter2(0, g0)
    scatter_sum(0, p0, fin)
    last.wait_recv()
    gin_ref[...] = (fin[...] + hdst[...]).astype(BF16)
    for cp in sent:
        cp.wait_send()


def on_device(tokens, cotangent, gate_weight, up_weight, down_weight, seq_ids, chosen, margins, counts):
    vmem = pl.BlockSpec(memory_space=pltpu.VMEM)
    smem = pl.BlockSpec(memory_space=pltpu.SMEM)
    hbm = pl.BlockSpec(memory_space=pl.ANY)
    dma = pltpu.SemaphoreType.DMA
    results = pl.pallas_call(
        kernel,
        out_shape=(
            pltpu.VMEM((ROWS, WIDTH), BF16),
            pltpu.VMEM((WIDTH, UNITS), BF16),
            pltpu.VMEM((WIDTH, UNITS), BF16),
            pltpu.VMEM((UNITS, WIDTH), BF16),
        ),
        in_specs=[hbm, hbm, hbm, hbm, hbm, smem, smem, smem, smem],
        out_specs=(vmem, vmem, vmem, vmem),
        scratch_shapes=[
            pltpu.VMEM((WIDTH, UNITS), BF16),
            pltpu.VMEM((WIDTH, UNITS), BF16),
            pltpu.VMEM((UNITS, WIDTH), BF16),
            pltpu.VMEM((2, 4, 4, ROWS, WIDTH), BF16),
            pltpu.VMEM((2, 4, 4, ROWS, WIDTH), BF16),
            pltpu.VMEM((ROWS, WIDTH), BF16),
            pltpu.VMEM((ROWS, WIDTH), BF16),
            pltpu.VMEM((3, CHUNK, UNITS), F32),
            pltpu.VMEM((2, 3, OWN, UNITS), BF16),
            pltpu.VMEM((2, 3, OWN, UNITS), BF16),
            pltpu.VMEM((2, 3, OWN, UNITS), F32),
            pltpu.VMEM((2, 3, OWN, UNITS), BF16),
            pltpu.VMEM((2, 3, OWN, UNITS), BF16),
            pltpu.VMEM((2, OWN, UNITS), F32),
            pltpu.VMEM((2, OWN, UNITS), F32),
            pltpu.VMEM((2, CHUNK, UNITS), BF16),
            pltpu.VMEM((2, 2, CHUNK, UNITS), BF16),
            pltpu.VMEM((CHUNK, WIDTH), F32),
            pltpu.VMEM((2, 4, 4, ROWS, WIDTH), BF16),
            pltpu.VMEM((2, 3, 4, ROWS, HALF), BF16),
            pltpu.VMEM((2, 3, 4, ROWS, HALF), BF16),
            pltpu.VMEM((4, ROWS, HALF), BF16),
            pltpu.VMEM((4, ROWS, HALF), BF16),
            pltpu.VMEM((2, 3, ROWS, HALF), BF16),
            pltpu.VMEM((4, ROWS, HALF), F32),
            pltpu.VMEM((4, ROWS, HALF), F32),
            pltpu.VMEM((2, 3, ROWS, HALF), F32),
            pltpu.VMEM((ROWS, WIDTH), F32),
            pltpu.VMEM((ROWS, WIDTH), F32),
            pltpu.VMEM((ROWS, WIDTH), F32),
            dma((5,)),
            dma((2,)),
            dma((2,)),
            dma((2, 2, 2, 2, 3)),
            dma((2, 2, 2, 2, 3)),
            dma((2, 3)),
            dma((2, 3)),
            dma((2, 3, 2)),
            dma((2, 3, 2)),
            dma((2,)),
            dma((2,)),
            dma((2, 2)),
            dma((2, 2)),
            dma((2, 2, 2, 3)),
            dma((2, 2, 2, 3)),
            dma((1,)),
            dma((1,)),
        ],
        compiler_params=pltpu.CompilerParams(
            collective_id=0, has_side_effects=True, vmem_limit_bytes=46 << 20
        ),
        cost_estimate=pl.CostEstimate(flops=15_000_000_000, bytes_accessed=22_000_000, transcendentals=0),
        name="simpo_backward",
    )(tokens, cotangent, gate_weight, up_weight, down_weight, seq_ids, chosen, margins, counts)
    return write_out(*results)


def write_out(*grads):
    count = len(grads)

    def body(*refs):
        sem = refs[-1]
        copies = [pltpu.make_async_copy(refs[i], refs[count + i], sem.at[i]) for i in range(count)]
        for cp in copies:
            cp.start()
        for cp in copies:
            cp.wait()

    return pl.pallas_call(
        body,
        out_shape=tuple(jax.ShapeDtypeStruct(g.shape, g.dtype) for g in grads),
        in_specs=[pl.BlockSpec(memory_space=pltpu.VMEM)] * count,
        out_specs=(pl.BlockSpec(memory_space=pl.ANY),) * count,
        scratch_shapes=[pltpu.SemaphoreType.DMA((count,))],
        compiler_params=pltpu.CompilerParams(vmem_limit_bytes=1 << 20),
        name="write_out",
    )(*grads)


def solution(mesh):
    return jax.shard_map(
        on_device,
        mesh=mesh,
        in_specs=(
            P(("out", "dep"), "inp"),
            P(("out", "dep"), "inp"),
            P("inp", ("out", "dep")),
            P("inp", ("out", "dep")),
            P(("out", "dep"), "inp"),
            P(("out", "dep")),
            P(("out", "dep")),
            P(),
            P(),
        ),
        out_specs=(
            P(("out", "dep"), "inp"),
            P("inp", ("out", "dep")),
            P("inp", ("out", "dep")),
            P(("out", "dep"), "inp"),
        ),
        check_vma=False,
    )
```

time: 95.1 us -> 84.3 us (0.89)
  local copies, waits for them, and re-layouts: 11 us -> 0 us
    unnamed x8 -> x0, local copies, waits for them, and re-layouts: 11 us -> none
    pallas_call x1 -> x2, Pallas kernels: 82.7 us -> 83.2 us  [the longest x1 78.9 us: on_device(): pl.pallas_call(kernel, out_shape=(pltpu.VMEM((ROWS, WIDTH), BF16), pltpu....]
where the time goes in v2:
time: 84.3 us; the launch traced here: 84 us
  Pallas kernels  83.2 us (99%)
    pallas_call x1, Pallas kernels, on_device(): pl.pallas_call(kernel, out_shape=(pltpu.VMEM((ROWS, WIDTH), BF16), pltpu....  78.9 us
    pallas_call x1, Pallas kernels, write_out(): pl.pallas_call(body, out_shape=tuple((jax.ShapeDtypeStruct(g.shape, g.dty...  4.31 us

profile of v2, /device:TPU:0, one launch (start us, length us, event | category | flops | bytes accessed | tf_op | source)
XLA Modules:
  0.0 84.0 jit_solution(4764279982275074014)
XLA Ops:
  0.6 78.9 %simpo_backward.1 = (bf16[16,2048]{1,0:T(8,128)(2,1)S(1)}, bf16[2048,896]{1,0:T(8,128)(2,1)S(1)}, bf16[2048,896]{1,0:T(8,128)(2,1)S(1)}, bf16[896,2048]{1,0:T(8,128)(2,1)S(1)}) custom-call(bf16[16,2048]{1,0:T(8,128)(2,1)} %tok_ref.1, bf16[16,2048]{1,0:T(8,128)(2,1)} %cot_ref.1, bf16[2048,896]{1,0:T(8,128)(2,1)} %gate_ref.1, bf16[2048,896]{1,0:T(8,128)(2,1)} %up_ref.1, ...), custom_call_target="tpu_custom_call" | custom-call | flops 15000000512 | bytes 22000000 | tf_op jit(solution)/shard_map/simpo_backward/pallas_call | solution.py:373
  79.6 4.3 %write_out.1 = (bf16[16,2048]{1,0:T(8,128)(2,1)}, bf16[2048,896]{1,0:T(8,128)(2,1)}, bf16[2048,896]{1,0:T(8,128)(2,1)}, bf16[896,2048]{1,0:T(8,128)(2,1)}) custom-call(bf16[16,2048]{1,0:T(8,128)(2,1)S(1)} %get-tuple-element.8.refs_0_, bf16[2048,896]{1,0:T(8,128)(2,1)S(1)} %get-tuple-element.9.refs_1_, bf16[2048,896]{1,0:T(8,128)(2,1)S(1)} %get-tuple-element.10.refs_2_, ...), custom_call_target="tpu_custom_call" | custom-call | tf_op jit(solution)/shard_map/write_out/pallas_call | solution.py:452

commit v3 on v2

v3 whole, which is shorter than its diff:
```python
import jax
import jax.numpy as jnp
from jax import lax
from jax.experimental import pallas as pl
from jax.experimental.pallas import tpu as pltpu
from jax.sharding import PartitionSpec as P

SIMPO_BETA = 2.5
LOSS_SCALE = 64.0
MESH = pl.DeviceIdType.MESH
BF16 = jnp.bfloat16
F32 = jnp.float32

WIDTH = 2048
HALF = 1024
UNITS = 896
ROWS = 16
TOKENS = 512
CHUNKS = ((0, 0), (128, 64), (256, 128), (384, 192))
ROWS_C = 128
SHARE = 64


def dot(left, right, dims):
    return lax.dot_general(left, right, (dims, ((), ())), preferred_element_type=F32)


def kernel(
    tok_ref,
    cot_ref,
    gate_ref,
    up_ref,
    down_ref,
    seq_ref,
    chosen_ref,
    margin_ref,
    count_ref,
    gin_ref,
    ggate_ref,
    gup_ref,
    gdown_ref,
    wgate,
    wup,
    wdn,
    tok,
    og,
    cot,
    ogown,
    part,
    xs,
    xr,
    summed,
    zs,
    zr,
    slope,
    swished,
    hid,
    gug,
    gpart,
    ra1,
    rb1,
    sa,
    sb,
    r2,
    sa1,
    sb1,
    r21,
    fin,
    hsrc,
    hdst,
    lsem,
    hsem_s,
    hsem_r,
    ag_s,
    ag_r,
    x_s,
    x_r,
    z_s,
    z_r,
    c_s,
    c_r,
    k_s,
    k_r,
    rs_s,
    rs_r,
    f_s,
    f_r,
):
    inp, x, dep = lax.axis_index("inp"), lax.axis_index("out"), lax.axis_index("dep")
    zl, core = inp // 2, inp % 2
    y, zh = dep // 2, dep % 2
    at_x = lambda d: (inp, (x + d) % 4, dep)
    at_y = lambda d: (inp, x, ((y + d) % 4) * 2 + zh)
    at_zh = (inp, x, y * 2 + 1 - zh)
    at_core = (zl * 2 + 1 - core, x, dep)
    at_zl = ((1 - zl) * 2 + core, x, dep)

    barrier = pltpu.get_barrier_semaphore()
    greeted = [at_x(1), at_x(2), at_x(3), at_y(1), at_y(2), at_y(3), at_zh, at_core, at_zl]
    for who in greeted:
        pl.semaphore_signal(barrier, inc=1, device_id=who, device_id_type=MESH)

    def load(src, dst, i):
        cp = pltpu.make_async_copy(src, dst, lsem.at[i])
        cp.start()
        return cp

    cot_load = load(cot_ref, cot, 0)
    tok_load = load(tok_ref, tok.at[0, (x + y) % 2, x // 2, x % 2, y // 2], 1)
    gate_load = load(gate_ref, wgate, 2)
    up_load = load(up_ref, wup, 3)
    down_load = load(down_ref, wdn, 4)

    sent = []

    def send(src, dst, s_sem, r_sem, who):
        cp = pltpu.make_async_remote_copy(
            src_ref=src, dst_ref=dst, send_sem=s_sem, recv_sem=r_sem, device_id=who, device_id_type=MESH
        )
        cp.start()
        sent.append(cp)
        return cp

    def arrived(cps):
        for cp in cps:
            cp.wait_recv()

    bufs = (tok, og)
    cols_of = (pl.ds(0, HALF), pl.ds(HALF, HALF))

    def block(ref, s, x, y):
        return ref.at[s, (x + y) % 2, x // 2, x % 2, y // 2]

    def of_x(ref, s, p, x, h):
        return ref.at[s, p, x // 2, x % 2, :, :, cols_of[h]]

    def of_y(ref, s, p, y, h):
        return ref.at[s, p, :, (y + p) % 2, y // 2, :, cols_of[h]]

    def ag1(a, s, own=None):
        got = []
        mine = block(bufs[a], s, x, y)
        for d in range(1, 4):
            for h in range(2):
                spot = mine.at[:, cols_of[h]]
                src = spot if own is None else own.at[:, cols_of[h]]
                who = at_y(d) if h == 0 else at_x(d)
                got.append(send(src, spot, ag_s.at[a, s, h, 0, d - 1], ag_r.at[a, s, h, 0, d - 1], who))
        return got

    def ag2(a, s, p):
        got = []
        for d in range(1, 4):
            for h in range(2):
                spot, who = (of_x(bufs[a], s, p, x, h), at_x(d)) if h == 0 else (of_y(bufs[a], s, p, y, h), at_y(d))
                got.append(send(spot, spot, ag_s.at[a, s, h, 1 + p, d - 1], ag_r.at[a, s, h, 1 + p, d - 1], who))
        return got

    pl.semaphore_wait(barrier, len(greeted))
    t01 = ag1(0, 0, tok_ref)
    tok_hop = send(tok_ref, block(tok, 1, x, y), hsem_s.at[0], hsem_r.at[0], at_zh)

    row = lax.broadcasted_iota(jnp.int32, (ROWS, 128), 0)
    margin = jnp.zeros((ROWS, 128), F32)
    length = jnp.ones((ROWS, 128), F32)
    polarity = jnp.zeros((ROWS, 128), F32)
    for t in range(ROWS):
        pair, pick = seq_ref[t], chosen_ref[t]
        margin = jnp.where(row == t, margin_ref[pair], margin)
        length = jnp.where(row == t, count_ref[2 * pair + pick].astype(F32), length)
        polarity = jnp.where(row == t, 1.0 - 2.0 * pick.astype(F32), polarity)
    weight = polarity * SIMPO_BETA * LOSS_SCALE * jax.nn.sigmoid(-margin) / length
    cot_load.wait()
    for j in range(WIDTH // 128):
        cols = pl.ds(j * 128, 128)
        value = (cot[:, cols].astype(F32) * weight).astype(BF16)
        ogown[:, cols] = value
        og[0, (x + y) % 2, x // 2, x % 2, y // 2, :, cols] = value
    og_hop = send(ogown, block(og, 1, x, y), hsem_s.at[1], hsem_r.at[1], at_zh)

    tok_load.wait()
    arrived(t01)
    t0a = ag2(0, 0, 0)
    arrived([tok_hop])
    t1p = ag1(0, 1)

    def tokens_of(ref, cs):
        if len(cs) == 2:
            return ref[cs[0] // 2].reshape(2 * ROWS_C, WIDTH)
        return ref[cs[0] // 2, cs[0] % 2].reshape(ROWS_C, WIDTH)

    xcp = {}
    zcp = {}

    def multiply(p, *cs):
        if p == 0:
            value = dot(tokens_of(tok, cs), wgate[...], ((1,), (0,)))
        elif p == 1:
            value = dot(tokens_of(tok, cs), wup[...], ((1,), (0,)))
        else:
            value = dot(tokens_of(og, cs), wdn[...], ((1,), (1,)))
        part[p, pl.ds(CHUNKS[cs[0]][0], len(cs) * ROWS_C)] = value
        for c in cs:
            row0, first = CHUNKS[c]
            share = pl.ds(first, SHARE)
            xs[p, share] = part[p, pl.ds(pl.multiple_of(row0 + (1 - core) * SHARE, SHARE), SHARE)].astype(BF16)
            xcp[c, p] = send(xs.at[p, share], xr.at[p, share], x_s.at[c, p], x_r.at[c, p], at_core)

    def pair_sum(p, *cs):
        for c in cs:
            xcp[c, p].wait_recv()
            row0, first = CHUNKS[c]
            share = pl.ds(first, SHARE)
            total = part[p, pl.ds(pl.multiple_of(row0 + core * SHARE, SHARE), SHARE)] + xr[p, share].astype(F32)
            summed[p, share] = total
            zs[p, share] = total.astype(BF16)
            zcp[c, p] = send(zs.at[p, share], zr.at[p, share], z_s.at[c, p], z_r.at[c, p], at_zl)

    def by_rows(c, body):
        row0, first = CHUNKS[c]

        def step(i, carry):
            body(
                pl.ds(pl.multiple_of(first + i * 16, 16), 16),
                pl.ds(pl.multiple_of(row0 + core * SHARE + i * 16, 16), 16),
            )
            return carry

        lax.fori_loop(0, SHARE // 16, step, 0)
        return pl.ds(pl.multiple_of(row0 + core * SHARE, SHARE), SHARE)

    def activate(c):
        zcp[c, 0].wait_recv()
        zcp[c, 1].wait_recv()

        def body(rows, at):
            gate_sum = summed[0, rows] + zr[0, rows].astype(F32)
            up_sum = summed[1, rows] + zr[1, rows].astype(F32)
            logistic = jax.nn.sigmoid(gate_sum)
            swish = gate_sum * logistic
            slope[rows] = up_sum * logistic * (1.0 + gate_sum * (1.0 - logistic))
            swished[rows] = swish
            hid[at] = (swish * up_sum).astype(BF16)

        spot = hid.at[by_rows(c, body)]
        return send(spot, spot, c_s.at[c], c_r.at[c], at_core)

    def act_grad(c):
        zcp[c, 2].wait_recv()

        def body(rows, at):
            hg = summed[2, rows] + zr[2, rows].astype(F32)
            gug[0, at] = (hg * slope[rows]).astype(BF16)
            gug[1, at] = (hg * swished[rows]).astype(BF16)

        spot = gug.at[:, by_rows(c, body)]
        return send(spot, spot, k_s.at[c], k_r.at[c], at_core)

    def grad_in(cs, cps, between=None):
        arrived(cps)
        span = pl.ds(CHUNKS[cs[0]][0], len(cs) * ROWS_C)
        planes = [(c // 2, c % 2) for c in cs]
        got = []
        for h in range(2):
            for q in range(2):
                wide = pl.ds(h * HALF + q * 512, 512)
                value = dot(gug[0, span], wgate[wide, :], ((1,), (1,)))
                value += dot(gug[1, span], wup[wide, :], ((1,), (1,)))
                value = value.astype(BF16).reshape(len(planes), 2, 2, 2, ROWS, 512)
                for i, (s, p) in enumerate(planes):
                    gpart[s, p, :, :, :, :, wide] = value[i]
            for d in range(1, 4):
                for s, p in planes:
                    if h == 0:
                        src, dst, who = of_x(gpart, s, p, (x + d) % 4, 0), ra1.at[s, p, d - 1], at_x(d)
                    else:
                        src, dst, who = of_y(gpart, s, p, (y + d) % 4, 1), rb1.at[s, p, d - 1], at_y(d)
                    got.append(send(src, dst, rs_s.at[s, h, p, d - 1], rs_r.at[s, h, p, d - 1], who))
            if h == 0 and between is not None:
                between()
        return got

    def first_sum(s, p, cps):
        arrived(cps)
        at_a, at_b = ((sa, sb), (sa1, sb1))[s]
        total = gpart[s, p, x // 2, x % 2, :, :, cols_of[0]].astype(F32)
        for d in range(3):
            total += ra1[s, p, d].astype(F32)
        at_a[p] = total.astype(at_a.dtype)
        total = gpart[s, p, :, (y + p) % 2, y // 2, :, cols_of[1]].astype(F32)
        for d in range(3):
            total += rb1[s, p, d].astype(F32)
        at_b[p] = total.astype(at_b.dtype)

    def pick_a(ref, y):
        return ref.at[(x + y) % 2, y // 2]

    def pick_b(ref, x):
        return ref.at[(x + y) % 2, x // 2]

    def scatter2(s):
        at_a, at_b, to = ((sa, sb, r2), (sa1, sb1, r21))[s]
        got = []
        for d in range(1, 4):
            sides = (
                (pick_a(at_a, (y + d) % 4), at_y(d)),
                (pick_b(at_b, (x + d) % 4), at_x(d)),
            )
            for h, (src, who) in enumerate(sides):
                got.append(send(src, to.at[h, d - 1], rs_s.at[s, h, 2, d - 1], rs_r.at[s, h, 2, d - 1], who))
        return got

    def scatter_sum(s, cps, out):
        arrived(cps)
        at_a, at_b, to = ((sa, sb, r2), (sa1, sb1, r21))[s]
        for h, own in enumerate((pick_a(at_a, y), pick_b(at_b, x))):
            total = own[...].astype(F32)
            for d in range(3):
                total += to[h, d].astype(F32)
            out[:, cols_of[h]] = total

    gate_load.wait()
    up_load.wait()
    arrived(t0a)
    arrived(t1p)
    t1a = ag2(0, 1, 0)
    multiply(0, 0)
    multiply(1, 0)
    t1b = ag2(0, 1, 1)
    pair_sum(0, 0)
    pair_sum(1, 0)
    arrived([og_hop])
    o1p = ag1(1, 1)
    arrived(t1a)
    multiply(0, 2)
    arrived(o1p)
    o1a = ag2(1, 1, 0)
    multiply(1, 2)
    o0p = ag1(1, 0, ogown)
    pair_sum(0, 2)
    pair_sum(1, 2)
    o1b = ag2(1, 1, 1)
    arrived(t1b)
    multiply(0, 3)
    multiply(1, 3)
    arrived(o0p)
    o0a = ag2(1, 0, 0)
    pair_sum(0, 3)
    pair_sum(1, 3)
    t0b = ag2(0, 0, 1)
    down_load.wait()
    arrived(o1a)
    multiply(2, 2)
    o0b = ag2(1, 0, 1)
    hid0 = activate(0)
    pair_sum(2, 2)
    arrived(o1b)
    multiply(2, 3)
    hid2 = activate(2)
    pair_sum(2, 3)
    arrived(o0a)
    multiply(2, 0)
    arrived(t0b)
    multiply(0, 1)
    pair_sum(2, 0)
    multiply(1, 1)
    pair_sum(0, 1)
    pair_sum(1, 1)
    hid3 = activate(3)
    k2 = act_grad(2)
    k3 = act_grad(3)
    arrived(o0b)
    multiply(2, 1)
    pair_sum(2, 1)
    later = []
    g23 = grad_in((2, 3), (k2, k3), lambda: later.append(act_grad(0)))
    g0 = grad_in((0,), later, lambda: later.append(activate(1)))
    k1 = act_grad(1)
    arrived([hid0, later[1], hid2, hid3])

    def down_tile(i, carry):
        rows = pl.ds(pl.multiple_of(i * 128, 128), 128)
        value = dot(hid[:, rows], og[...].reshape(TOKENS, WIDTH), ((0,), (0,)))
        gdown_ref[rows, :] = value.astype(BF16)
        return carry

    lax.fori_loop(0, 4, down_tile, 0)
    p1 = []

    def between():
        first_sum(1, 0, g23[0::2])
        first_sum(1, 1, g23[1::2])
        p1.extend(scatter2(1))

    g1 = grad_in((1,), (k1,), between)

    def gate_tile(i, carry):
        rows = pl.ds(pl.multiple_of(i * 256, 256), 256)
        left = tok[:, :, :, :, :, :, rows].reshape(TOKENS, 256)
        value = dot(left, jnp.concatenate([gug[0], gug[1]], axis=1), ((0,), (0,)))
        ggate_ref[rows, :] = value[:, :UNITS].astype(BF16)
        gup_ref[rows, :] = value[:, UNITS:].astype(BF16)
        return carry

    first_sum(0, 0, g0)
    lax.fori_loop(0, 5, gate_tile, 0)
    first_sum(0, 1, g1)
    p0 = scatter2(0)
    scatter_sum(1, p1, hsrc)
    last = send(hsrc, hdst, f_s.at[0], f_r.at[0], at_zh)
    lax.fori_loop(5, 8, gate_tile, 0)
    lax.fori_loop(4, UNITS // 128, down_tile, 0)
    scatter_sum(0, p0, fin)
    last.wait_recv()
    gin_ref[...] = (fin[...] + hdst[...]).astype(BF16)
    for cp in sent:
        cp.wait_send()


def on_device(tokens, cotangent, gate_weight, up_weight, down_weight, seq_ids, chosen, margins, counts):
    vmem = pl.BlockSpec(memory_space=pltpu.VMEM)
    smem = pl.BlockSpec(memory_space=pltpu.SMEM)
    hbm = pl.BlockSpec(memory_space=pl.ANY)
    dma = pltpu.SemaphoreType.DMA
    results = pl.pallas_call(
        kernel,
        out_shape=(
            pltpu.VMEM((ROWS, WIDTH), BF16),
            pltpu.VMEM((WIDTH, UNITS), BF16),
            pltpu.VMEM((WIDTH, UNITS), BF16),
            pltpu.VMEM((UNITS, WIDTH), BF16),
        ),
        in_specs=[hbm, hbm, hbm, hbm, hbm, smem, smem, smem, smem],
        out_specs=(vmem, vmem, vmem, vmem),
        scratch_shapes=[
            pltpu.VMEM((WIDTH, UNITS), BF16),
            pltpu.VMEM((WIDTH, UNITS), BF16),
            pltpu.VMEM((UNITS, WIDTH), BF16),
            pltpu.VMEM((2, 2, 2, 2, 2, ROWS, WIDTH), BF16),
            pltpu.VMEM((2, 2, 2, 2, 2, ROWS, WIDTH), BF16),
            pltpu.VMEM((ROWS, WIDTH), BF16),
            pltpu.VMEM((ROWS, WIDTH), BF16),
            pltpu.VMEM((3, TOKENS, UNITS), F32),
            pltpu.VMEM((3, 256, UNITS), BF16),
            pltpu.VMEM((3, 256, UNITS), BF16),
            pltpu.VMEM((3, 256, UNITS), F32),
            pltpu.VMEM((3, 256, UNITS), BF16),
            pltpu.VMEM((3, 256, UNITS), BF16),
            pltpu.VMEM((256, UNITS), F32),
            pltpu.VMEM((256, UNITS), F32),
            pltpu.VMEM((TOKENS, UNITS), BF16),
            pltpu.VMEM((2, TOKENS, UNITS), BF16),
            pltpu.VMEM((2, 2, 2, 2, 2, ROWS, WIDTH), BF16),
            pltpu.VMEM((2, 2, 3, 2, ROWS, HALF), BF16),
            pltpu.VMEM((2, 2, 3, 2, ROWS, HALF), BF16),
            pltpu.VMEM((2, 2, ROWS, HALF), BF16),
            pltpu.VMEM((2, 2, ROWS, HALF), BF16),
            pltpu.VMEM((2, 3, ROWS, HALF), BF16),
            pltpu.VMEM((2, 2, ROWS, HALF), BF16),
            pltpu.VMEM((2, 2, ROWS, HALF), BF16),
            pltpu.VMEM((2, 3, ROWS, HALF), BF16),
            pltpu.VMEM((ROWS, WIDTH), F32),
            pltpu.VMEM((ROWS, WIDTH), F32),
            pltpu.VMEM((ROWS, WIDTH), F32),
            dma((5,)),
            dma((2,)),
            dma((2,)),
            dma((2, 2, 2, 3, 3)),
            dma((2, 2, 2, 3, 3)),
            dma((4, 3)),
            dma((4, 3)),
            dma((4, 3)),
            dma((4, 3)),
            dma((4,)),
            dma((4,)),
            dma((4,)),
            dma((4,)),
            dma((2, 2, 3, 3)),
            dma((2, 2, 3, 3)),
            dma((1,)),
            dma((1,)),
        ],
        compiler_params=pltpu.CompilerParams(
            collective_id=0, has_side_effects=True, vmem_limit_bytes=46 << 20
        ),
        cost_estimate=pl.CostEstimate(flops=15_000_000_000, bytes_accessed=22_000_000, transcendentals=0),
        name="simpo_backward",
    )(tokens, cotangent, gate_weight, up_weight, down_weight, seq_ids, chosen, margins, counts)
    return write_out(*results)


def write_out(*grads):
    count = len(grads)

    def body(*refs):
        sem = refs[-1]
        copies = [pltpu.make_async_copy(refs[i], refs[count + i], sem.at[i]) for i in range(count)]
        for cp in copies:
            cp.start()
        for cp in copies:
            cp.wait()

    return pl.pallas_call(
        body,
        out_shape=tuple(jax.ShapeDtypeStruct(g.shape, g.dtype) for g in grads),
        in_specs=[pl.BlockSpec(memory_space=pltpu.VMEM)] * count,
        out_specs=(pl.BlockSpec(memory_space=pl.ANY),) * count,
        scratch_shapes=[pltpu.SemaphoreType.DMA((count,))],
        compiler_params=pltpu.CompilerParams(vmem_limit_bytes=1 << 20),
        name="write_out",
    )(*grads)


def solution(mesh):
    return jax.shard_map(
        on_device,
        mesh=mesh,
        in_specs=(
            P(("out", "dep"), "inp"),
            P(("out", "dep"), "inp"),
            P("inp", ("out", "dep")),
            P("inp", ("out", "dep")),
            P(("out", "dep"), "inp"),
            P(("out", "dep")),
            P(("out", "dep")),
            P(),
            P(),
        ),
        out_specs=(
            P(("out", "dep"), "inp"),
            P("inp", ("out", "dep")),
            P("inp", ("out", "dep")),
            P(("out", "dep"), "inp"),
        ),
        check_vma=False,
    )
```

time: 84.3 us -> 77.6 us (0.921)
  Pallas kernels: 83.2 us -> 76.7 us
    pallas_call x1, Pallas kernels: 78.9 us -> 72.4 us  [on_device(): pl.pallas_call(kernel, out_shape=(pltpu.VMEM((ROWS, WIDTH), BF16), pltpu....]
where the time goes in v3:
time: 77.6 us; the launch traced here: 77.5 us
  Pallas kernels  76.7 us (99%)
  between operations  0.8 us (1%)
    pallas_call x1, Pallas kernels, on_device(): pl.pallas_call(kernel, out_shape=(pltpu.VMEM((ROWS, WIDTH), BF16), pltpu....  72.4 us
    pallas_call x1, Pallas kernels, write_out(): pl.pallas_call(body, out_shape=tuple((jax.ShapeDtypeStruct(g.shape, g.dty...  4.31 us

profile of v3, /device:TPU:0, one launch (start us, length us, event | category | flops | bytes accessed | tf_op | source)
XLA Modules:
  0.0 77.5 jit_solution(3121253621756996894)
XLA Ops:
  0.6 72.4 %simpo_backward.1 = (bf16[16,2048]{1,0:T(8,128)(2,1)S(1)}, bf16[2048,896]{1,0:T(8,128)(2,1)S(1)}, bf16[2048,896]{1,0:T(8,128)(2,1)S(1)}, bf16[896,2048]{1,0:T(8,128)(2,1)S(1)}) custom-call(bf16[16,2048]{1,0:T(8,128)(2,1)} %tok_ref.1, bf16[16,2048]{1,0:T(8,128)(2,1)} %cot_ref.1, bf16[2048,896]{1,0:T(8,128)(2,1)} %gate_ref.1, bf16[2048,896]{1,0:T(8,128)(2,1)} %up_ref.1, ...), custom_call_target="tpu_custom_call" | custom-call | flops 15000000512 | bytes 22000000 | tf_op jit(solution)/shard_map/simpo_backward/pallas_call | solution.py:425
  73.1 4.3 %write_out.1 = (bf16[16,2048]{1,0:T(8,128)(2,1)}, bf16[2048,896]{1,0:T(8,128)(2,1)}, bf16[2048,896]{1,0:T(8,128)(2,1)}, bf16[896,2048]{1,0:T(8,128)(2,1)}) custom-call(bf16[16,2048]{1,0:T(8,128)(2,1)S(1)} %get-tuple-element.8.refs_0_, bf16[2048,896]{1,0:T(8,128)(2,1)S(1)} %get-tuple-element.9.refs_1_, bf16[2048,896]{1,0:T(8,128)(2,1)S(1)} %get-tuple-element.10.refs_2_, ...), custom_call_target="tpu_custom_call" | custom-call | tf_op jit(solution)/shard_map/write_out/pallas_call | solution.py:503

commit v4 on v3

--- a/solution.py
+++ b/solution.py
@@ -326,9 +326,9 @@
     t1a = ag2(0, 1, 0)
     multiply(0, 0)
     multiply(1, 0)
-    t1b = ag2(0, 1, 1)
     pair_sum(0, 0)
     pair_sum(1, 0)
+    t1b = ag2(0, 1, 1)
     arrived([og_hop])
     o1p = ag1(1, 1)
     arrived(t1a)
@@ -403,12 +403,12 @@
         return carry
 
     first_sum(0, 0, g0)
-    lax.fori_loop(0, 5, gate_tile, 0)
+    lax.fori_loop(0, 4, gate_tile, 0)
     first_sum(0, 1, g1)
     p0 = scatter2(0)
     scatter_sum(1, p1, hsrc)
     last = send(hsrc, hdst, f_s.at[0], f_r.at[0], at_zh)
-    lax.fori_loop(5, 8, gate_tile, 0)
+    lax.fori_loop(4, 8, gate_tile, 0)
     lax.fori_loop(4, UNITS // 128, down_tile, 0)
     scatter_sum(0, p0, fin)
     last.wait_recv()
@@ -494,7 +494,12 @@
 
     def body(*refs):
         sem = refs[-1]
-        copies = [pltpu.make_async_copy(refs[i], refs[count + i], sem.at[i]) for i in range(count)]
+        copies = [pltpu.make_async_copy(refs[0], refs[count], sem.at[0, 0])]
+        for i in range(1, count):
+            part = grads[i].shape[0] // 4
+            for j in range(4):
+                rows = pl.ds(j * part, part)
+                copies.append(pltpu.make_async_copy(refs[i].at[rows], refs[count + i].at[rows], sem.at[i, j]))
         for cp in copies:
             cp.start()
         for cp in copies:
@@ -505,7 +510,7 @@
         out_shape=tuple(jax.ShapeDtypeStruct(g.shape, g.dtype) for g in grads),
         in_specs=[pl.BlockSpec(memory_space=pltpu.VMEM)] * count,
         out_specs=(pl.BlockSpec(memory_space=pl.ANY),) * count,
-        scratch_shapes=[pltpu.SemaphoreType.DMA((count,))],
+        scratch_shapes=[pltpu.SemaphoreType.DMA((count, 4))],
         compiler_params=pltpu.CompilerParams(vmem_limit_bytes=1 << 20),
         name="write_out",
     )(*grads)

time: 77.6 us -> 79.3 us (1.022)
  Pallas kernels: 76.7 us -> 78.4 us
    pallas_call x1, Pallas kernels: 72.4 us -> 74.1 us  [on_device(): pl.pallas_call(kernel, out_shape=(pltpu.VMEM((ROWS, WIDTH), BF16), pltpu....]
where the time goes in v4:
time: 79.3 us; the launch traced here: 79.2 us
  Pallas kernels  78.4 us (99%)
  between operations  0.8 us (1%)
    pallas_call x1, Pallas kernels, on_device(): pl.pallas_call(kernel, out_shape=(pltpu.VMEM((ROWS, WIDTH), BF16), pltpu....  74.1 us
    pallas_call x1, Pallas kernels, write_out(): pl.pallas_call(body, out_shape=tuple((jax.ShapeDtypeStruct(g.shape, g.dty...  4.25 us

profile of v4, /device:TPU:0, one launch (start us, length us, event | category | flops | bytes accessed | tf_op | source)
XLA Modules:
  0.0 79.2 jit_solution(16375095085879402393)
XLA Ops:
  0.6 74.1 %simpo_backward.1 = (bf16[16,2048]{1,0:T(8,128)(2,1)S(1)}, bf16[2048,896]{1,0:T(8,128)(2,1)S(1)}, bf16[2048,896]{1,0:T(8,128)(2,1)S(1)}, bf16[896,2048]{1,0:T(8,128)(2,1)S(1)}) custom-call(bf16[16,2048]{1,0:T(8,128)(2,1)} %tok_ref.1, bf16[16,2048]{1,0:T(8,128)(2,1)} %cot_ref.1, bf16[2048,896]{1,0:T(8,128)(2,1)} %gate_ref.1, bf16[2048,896]{1,0:T(8,128)(2,1)} %up_ref.1, ...), custom_call_target="tpu_custom_call" | custom-call | flops 15000000512 | bytes 22000000 | tf_op jit(solution)/shard_map/simpo_backward/pallas_call | solution.py:425
  74.8 4.3 %write_out.1 = (bf16[16,2048]{1,0:T(8,128)(2,1)}, bf16[2048,896]{1,0:T(8,128)(2,1)}, bf16[2048,896]{1,0:T(8,128)(2,1)}, bf16[896,2048]{1,0:T(8,128)(2,1)}) custom-call(bf16[16,2048]{1,0:T(8,128)(2,1)S(1)} %get-tuple-element.8.refs_0_, bf16[2048,896]{1,0:T(8,128)(2,1)S(1)} %get-tuple-element.9.refs_1_, bf16[2048,896]{1,0:T(8,128)(2,1)S(1)} %get-tuple-element.10.refs_2_, ...), custom_call_target="tpu_custom_call" | custom-call | tf_op jit(solution)/shard_map/write_out/pallas_call | solution.py:508

commit v5 on v3

--- a/solution.py
+++ b/solution.py
@@ -317,7 +317,7 @@
             total = own[...].astype(F32)
             for d in range(3):
                 total += to[h, d].astype(F32)
-            out[:, cols_of[h]] = total
+            out[:, cols_of[h]] = total.astype(out.dtype)
 
     gate_load.wait()
     up_load.wait()
@@ -412,7 +412,7 @@
     lax.fori_loop(4, UNITS // 128, down_tile, 0)
     scatter_sum(0, p0, fin)
     last.wait_recv()
-    gin_ref[...] = (fin[...] + hdst[...]).astype(BF16)
+    gin_ref[...] = (fin[...] + hdst[...].astype(F32)).astype(BF16)
     for cp in sent:
         cp.wait_send()
 
@@ -460,8 +460,8 @@
             pltpu.VMEM((2, 2, ROWS, HALF), BF16),
             pltpu.VMEM((2, 3, ROWS, HALF), BF16),
             pltpu.VMEM((ROWS, WIDTH), F32),
-            pltpu.VMEM((ROWS, WIDTH), F32),
-            pltpu.VMEM((ROWS, WIDTH), F32),
+            pltpu.VMEM((ROWS, WIDTH), BF16),
+            pltpu.VMEM((ROWS, WIDTH), BF16),
             dma((5,)),
             dma((2,)),
             dma((2,)),

time: 77.6 us -> 76.9 us (level)
  no operation moved by 1% of the time
where the time goes in v5:
time: 76.9 us; the launch traced here: 76.8 us
  Pallas kernels  76 us (99%)
  between operations  0.8 us (1%)
    pallas_call x1, Pallas kernels, on_device(): pl.pallas_call(kernel, out_shape=(pltpu.VMEM((ROWS, WIDTH), BF16), pltpu....  71.7 us
    pallas_call x1, Pallas kernels, write_out(): pl.pallas_call(body, out_shape=tuple((jax.ShapeDtypeStruct(g.shape, g.dty...  4.31 us

profile of v5, /device:TPU:0, one launch (start us, length us, event | category | flops | bytes accessed | tf_op | source)
XLA Modules:
  0.0 76.8 jit_solution(17956364249082395975)
XLA Ops:
  0.6 71.7 %simpo_backward.1 = (bf16[16,2048]{1,0:T(8,128)(2,1)S(1)}, bf16[2048,896]{1,0:T(8,128)(2,1)S(1)}, bf16[2048,896]{1,0:T(8,128)(2,1)S(1)}, bf16[896,2048]{1,0:T(8,128)(2,1)S(1)}) custom-call(bf16[16,2048]{1,0:T(8,128)(2,1)} %tok_ref.1, bf16[16,2048]{1,0:T(8,128)(2,1)} %cot_ref.1, bf16[2048,896]{1,0:T(8,128)(2,1)} %gate_ref.1, bf16[2048,896]{1,0:T(8,128)(2,1)} %up_ref.1, ...), custom_call_target="tpu_custom_call" | custom-call | flops 15000000512 | bytes 22000000 | tf_op jit(solution)/shard_map/simpo_backward/pallas_call | solution.py:425
  72.4 4.3 %write_out.1 = (bf16[16,2048]{1,0:T(8,128)(2,1)}, bf16[2048,896]{1,0:T(8,128)(2,1)}, bf16[2048,896]{1,0:T(8,128)(2,1)}, bf16[896,2048]{1,0:T(8,128)(2,1)}) custom-call(bf16[16,2048]{1,0:T(8,128)(2,1)S(1)} %get-tuple-element.8.refs_0_, bf16[2048,896]{1,0:T(8,128)(2,1)S(1)} %get-tuple-element.9.refs_1_, bf16[2048,896]{1,0:T(8,128)(2,1)S(1)} %get-tuple-element.10.refs_2_, ...), custom_call_target="tpu_custom_call" | custom-call | tf_op jit(solution)/shard_map/write_out/pallas_call | solution.py:503
